TPU v7x, 32 devices: a whole 2x2x4 slice. The times are simulated.
32 devices in a mesh: grp: 2 (over y), row: 4 (over x, core), col: 4 (over z).
Axes of the slice: x: 2, y: 2, z: 4, core: 2. Of those that a mesh axis runs over, the one named last changes fastest.
Arguments:
- density: float32 [32, 4, 2, 128, 128], P(('grp', 'row'), 'col'), parts along dimension 0, as said below
- slot_cols: int32 [32, 4, 2], P('grp'), parts along dimension 0, may hold values from -1 to 15, as said below
- block_at: int32 [32], P('grp'), parts along dimension 0, may hold values from 0 to 15, as said below
Outputs:
- purified: float32 [32, 4, 2, 128, 128], P(('grp', 'row'), 'col'), parts along dimension 0
There are 2 independent parts, one for each index of `grp`. A program takes and returns all parts, laid end to end along the dimension named above; each array names one. Nothing has to cross between parts.
Inputs may be any that keep to these rules, and one draw needn't show every extreme that they name: block_at is a permutation of the 16 block ids; position p of a block fixes the device along `row` that holds its block row (p // 4) and the column group of its block column (p // 4). slot_cols[p, c, u] is -1 or the id of a block whose position lies in column group c; in each row and group the live slots come first and name distinct blocks; slot 0 of a row in its own group is the row's own block; the pattern is symmetric: block j is stored in the row of block i exactly when block i is stored in the row of block j. `density`: the tile in slot (p, c, u) is block (block_at[p], slot_cols[p, c, u]) of a symmetric matrix, so the stored tile of block (j, i) is its transpose; tiles of empty slots are zero.
All inputs are finite; a program needn't handle non-finite values.
Results may differ from a plain program's by a relative error of at most 0.0003.
Values sent between devices are 32-bit elements; how exact they have to be, the bound alone decides.
A program may use at most 128 MiB of HBM per device.

v0:
```python
import jax
import jax.numpy as jnp
from jax import lax
from jax.sharding import PartitionSpec as P

HIGHEST = lax.Precision.HIGHEST


def positions(block_at, block_ids):
    nblocks = block_at.shape[0]
    order_ids = jnp.arange(nblocks, dtype=jnp.int32)
    return jnp.max(jnp.where(block_at == block_ids[..., None], order_ids, 0), axis=-1)


def on_device(density, slot_cols, block_at):
    row_count, _, slot_count, tile_size, _ = density.shape
    nblocks, ngroups, _ = slot_cols.shape
    first_row = lax.axis_index("row") * row_count
    my_group = lax.axis_index("col")
    my_cols = lax.dynamic_slice_in_dim(slot_cols, first_row, row_count, 0)
    is_live = my_cols >= 0
    target_pos = positions(block_at, my_cols)
    own_ids = lax.dynamic_index_in_dim(my_cols, my_group, 1, keepdims=False)
    panel_ids = lax.dynamic_index_in_dim(slot_cols, my_group, 1, keepdims=False)
    slot_ids = jnp.arange(slot_count, dtype=jnp.int32)
    candidates = panel_ids[target_pos]
    matches = candidates[:, :, :, None, :] == own_ids[:, None, None, :, None]
    matches = matches & (own_ids >= 0)[:, None, None, :, None] & is_live[:, :, :, None, None]
    present = jnp.any(matches, axis=-1)
    chosen_slot = jnp.max(jnp.where(matches, slot_ids, 0), axis=-1)
    flat_index = target_pos[..., None] * slot_count + chosen_slot
    own_tiles = density[:, 0]

    def slot_terms(left_side, flat_panel, group_count):
        summed = jnp.zeros((group_count, row_count, slot_count, tile_size, tile_size), jnp.float32)
        for kslot in range(slot_count):
            selected = jnp.take(flat_panel, flat_index[..., kslot], axis=0)
            selected = jnp.where(present[..., kslot, None, None], selected, 0.0)
            summed = summed + jnp.einsum(
                "pab,pcudb->cpuad", left_side[:, kslot], selected, precision=HIGHEST
            )
        return summed

    gathered = lax.all_gather(density, "row", axis=0, tiled=True)
    flat_density = gathered.reshape(nblocks * slot_count, tile_size, tile_size)
    square_part = lax.psum_scatter(
        slot_terms(own_tiles, flat_density, lax.axis_size("col") * 1),
        "col",
        scatter_dimension=0,
        tiled=True,
    )
    square = square_part.reshape(row_count, slot_count, tile_size, tile_size)
    square_gathered = lax.all_gather(square, "row", axis=0, tiled=True)
    flat_square = square_gathered.reshape(nblocks * slot_count, tile_size, tile_size)
    cubic_part = lax.psum_scatter(
        slot_terms(square, flat_density, lax.axis_size("col") * 1)
        + slot_terms(own_tiles, flat_square, lax.axis_size("col") * 1),
        "col",
        scatter_dimension=0,
        tiled=True,
    )
    purified = 3.0 * square - cubic_part.reshape(row_count, slot_count, tile_size, tile_size)
    return purified.reshape(row_count, 1, slot_count, tile_size, tile_size)


def solution(mesh):
    in_specs = (P(("grp", "row"), "col", None, None, None), P("grp", None, None), P("grp"))
    out_specs = P(("grp", "row"), "col", None, None, None)
    return jax.shard_map(
        on_device, mesh=mesh, in_specs=in_specs, out_specs=out_specs, check_vma=False
    )
```

profile of v0, /device:TPU:0, one launch (start us, length us, event | category | flops | bytes accessed | tf_op | source)
XLA Modules:
  0.0 266.6 jit_solution(3669405202114589186)
XLA Ops:
  6.5 0.7 all-gather.4.cloned.1.call-update
  7.3 0.0 all-reduce.5.cloned.1.call-start
  7.3 1.1 copy.131
  8.4 0.8 broadcast_compare_fusion
  9.2 0.1 copy.102
  9.3 0.1 copy.96
  9.4 0.9 select_reduce_fusion.1
  10.3 0.1 copy.98
  10.4 0.1 reshape.106
  10.5 0.7 dynamic-slice_bitcast_fusion.1
  11.2 0.1 copy.99
  11.3 0.6 gather_fusion
  11.9 0.1 copy.101
  12.0 0.8 broadcast_compare_fusion.1
  12.8 0.1 fusion.43
  12.9 0.1 copy.108
  13.0 0.1 copy.103
  13.2 0.1 copy.109
  13.3 0.1 copy.105
  13.5 0.1 copy.110
  13.6 0.1 reshape.127
  13.7 0.1 copy.106
  13.8 0.1 reshape.123
  13.9 20.3 %all-gather.4.cloned.1.call-done = f32[16,1,2,128,128]{4,3,2,1,0:T(8,128)} async-done(((f32[4,1,2,128,128]{4,3,2,1,0:T(8,128)}), f32[16,1,2,128,128]{4,3,2,1,0:T(8,128)}) %all-gather.4.cloned.1.call-update) | async-done | bytes 2097168 | tf_op jit(solution)/shard_map/all_gather | solution.py:44
  34.2 2.3 gather_fusion.1
  36.5 3.6 %gather_fusion.2 = f32[32,128,128]{2,1,0:T(8,128)} fusion(f32[32,128,128]{2,1,0:T(8,128)} %bitcast.96, s32[1024]{0:T(1024)S(1)} %pad_clamp_fusion), kind=kCustom, calls=%fused_computation.1.clone | custom fusion | bytes 4194432 | tf_op jit(solution)/shard_map/jit(_take)/gather | solution.py:37
  40.1 2.1 fusion.3
  42.2 3.5 %add_bitcast_fusion.1 = f32[4,4,2,128,128]{3,4,2,0,1:T(8,128)} fusion(f32[4,4,2,128,128]{4,3,2,1,0:T(8,128)S(1)} %fusion.3, f32[4,4,2,128,128]{4,3,2,1,0:T(8,128)S(1)} %bitcast.92, pred[4,4,2]{2,1,0:T(4,128)(4,1)S(1)} %copy.109, pred[4,4,2]{2,1,0:T(4,128)(4,1)S(1)} %copy.108, f32[4,2,128,128]{3,2,0,1:T(8,128)S(1)} %bitcast.100), kind=kOutput, calls=%fused_computation.12 | convolution fusion | flops 806879232 | bytes 6557696 | tf_op jit(solution)/shard_map/pab,pcudb->cpuad/dot_general | solution.py:39
  45.7 0.0 all-reduce.5.cloned.1.call-update
  45.7 0.0 all-gather.6.cloned.1.call-start
  45.8 0.6 copy-done.4
  46.4 0.6 dynamic-slice
  47.0 85.4 %all-reduce.5.cloned.1.call-done = f32[4,4,2,128,128]{3,4,2,0,1:T(8,128)} async-done(((f32[4,4,2,128,128]{3,4,2,0,1:T(8,128)}), f32[4,4,2,128,128]{3,4,2,0,1:T(8,128)}) %all-reduce.5.cloned.1.call-update) | async-done | bytes 2097168
  132.4 1.7 constant_dynamic-slice_fusion
  134.1 1.0 copy.113
  135.1 0.0 all-gather.6.cloned.1.call-update
  135.1 0.2 all-reduce.7.cloned.1.call-start
  135.4 1.0 copy.111
  136.4 5.1 %fusion.4 = f32[4,4,2,128,128]{4,3,2,1,0:T(8,128)} fusion(f32[4,4,2,128,128]{4,3,2,1,0:T(8,128)} %bitcast.91, pred[4,4,2]{2,1,0:T(4,128)(4,1)S(1)} %copy.109, pred[4,4,2]{2,1,0:T(4,128)(4,1)S(1)} %copy.108, f32[4,2,128,128]{3,2,0,1:T(8,128)} %bitcast.103), kind=kOutput, calls=%fused_computation.15 | convolution fusion | flops 806354944 | bytes 4456512 | tf_op jit(solution)/shard_map/pab,pcudb->cpuad/dot_general | solution.py:39
  141.5 3.4 %fusion.2 = f32[4,4,2,128,128]{4,3,2,1,0:T(8,128)} fusion(f32[4,4,2,128,128]{4,3,2,1,0:T(8,128)S(1)} %bitcast.90, pred[4,4,2]{2,1,0:T(4,128)(4,1)S(1)} %copy.105, pred[4,4,2]{2,1,0:T(4,128)(4,1)S(1)} %copy.103, f32[4,2,128,128]{3,2,0,1:T(8,128)S(1)} %bitcast.104), kind=kOutput, calls=%fused_computation.13 | convolution fusion | flops 806354944 | bytes 4460544 | tf_op jit(solution)/shard_map/pab,pcudb->cpuad/dot_general | solution.py:39
  144.8 12.0 %all-gather.6.cloned.1.call-done = f32[1,16,2,128,128]{4,3,2,0,1:T(8,128)} async-done(((f32[1,4,2,128,128]{4,3,2,0,1:T(8,128)}), f32[1,16,2,128,128]{4,3,2,0,1:T(8,128)}) %all-gather.6.cloned.1.call-update) | async-done | bytes 2097168 | tf_op jit(solution)/shard_map/all_gather | solution.py:53
  156.8 3.6 %gather_fusion.4 = f32[32,128,128]{2,1,0:T(8,128)} fusion(f32[32,128,128]{2,1,0:T(8,128)} %bitcast.97, s32[1024]{0:T(1024)S(1)} %pad_clamp_fusion), kind=kCustom, calls=%fused_computation.3.clone | custom fusion | bytes 4194432 | tf_op jit(solution)/shard_map/jit(_take)/gather | solution.py:37
  160.5 2.3 gather_fusion.3
  162.8 3.8 %fusion = f32[4,4,2,128,128]{4,3,2,1,0:T(8,128)S(1)} fusion(f32[4,4,2,128,128]{4,3,2,1,0:T(8,128)} %bitcast.94, pred[4,4,2]{2,1,0:T(4,128)(4,1)S(1)} %copy.109, pred[4,4,2]{2,1,0:T(4,128)(4,1)S(1)} %copy.108, f32[4,2,128,128]{3,2,0,1:T(8,128)S(1)} %bitcast.101), kind=kOutput, calls=%fused_computation.6 | convolution fusion | flops 806354944 | bytes 4460544 | tf_op jit(solution)/shard_map/pab,pcudb->cpuad/dot_general | solution.py:39
  166.6 3.9 %add_bitcast_fusion = f32[4,4,2,128,128]{3,4,2,0,1:T(8,128)} fusion(f32[4,4,2,128,128]{4,3,2,1,0:T(8,128)S(1)} %fusion, f32[4,4,2,128,128]{4,3,2,1,0:T(8,128)S(1)} %copy-done.2, f32[4,4,2,128,128]{4,3,2,1,0:T(8,128)S(1)} %copy-done.1, f32[4,4,2,128,128]{4,3,2,1,0:T(8,128)S(1)} %bitcast.93, pred[4,4,2]{2,1,0:T(4,128)(4,1)S(1)} %copy.105, ...), kind=kOutput, calls=%fused_computation.11 | convolution fusion | flops 807927808 | bytes 10752000 | tf_op jit(solution)/shard_map/pab,pcudb->cpuad/dot_general | solution.py:39
  170.6 86.7 %all-reduce.7.cloned.1.call-done = f32[4,4,2,128,128]{3,4,2,0,1:T(8,128)} async-done(((f32[4,4,2,128,128]{3,4,2,0,1:T(8,128)}), f32[4,4,2,128,128]{3,4,2,0,1:T(8,128)}) %all-reduce.7.cloned.1.call-update) | async-done | bytes 2097168
  257.2 1.9 fusion.30
  259.1 1.0 copy.117
  (21 shorter events, 0.1 us)
Async XLA Ops:
  6.5 27.7 %all-gather.4.cloned.1.call-start = ((), (), s32[]{:S(2)}) async-start(), calls=%async_computation | async-start | bytes 2621440 | tf_op jit(solution)/shard_map/all_gather | solution.py:44
  7.3 125.2 %all-reduce.5.cloned.1.call-start = ((), (), s32[]{:S(2)}) async-start(), calls=%async_computation.2 | async-start | bytes 4194304
  40.1 2.1 copy-start
  45.7 0.7 copy-start.4
  45.7 111.1 %all-gather.6.cloned.1.call-start = ((), (), s32[]{:S(2)}) async-start(), calls=%async_computation.1 | async-start | bytes 2621440 | tf_op jit(solution)/shard_map/all_gather | solution.py:53
  135.1 122.1 %all-reduce.7.cloned.1.call-start = ((), (), s32[]{:S(2)}) async-start(), calls=%async_computation.3 | async-start | bytes 4194304
  136.4 5.1 %copy-start.3 = (f32[1,4,2,128,128]{4,3,1,2,0:T(8,128)S(1)}, f32[1,4,2,128,128]{4,3,1,2,0:T(8,128)}, u32[]{:S(2)}) copy-start(f32[1,4,2,128,128]{4,3,1,2,0:T(8,128)} %copy.111) | copy-start | bytes 1572868
  162.7 3.9 %copy-start.1 = (f32[4,4,2,128,128]{4,3,2,1,0:T(8,128)S(1)}, f32[4,4,2,128,128]{4,3,2,1,0:T(8,128)}, u32[]{:S(2)}) copy-start(f32[4,4,2,128,128]{4,3,2,1,0:T(8,128)} %fusion.4) | copy-start | bytes 6291460
  162.7 3.9 %copy-start.2 = (f32[4,4,2,128,128]{4,3,2,1,0:T(8,128)S(1)}, f32[4,4,2,128,128]{4,3,2,1,0:T(8,128)}, u32[]{:S(2)}) copy-start(f32[4,4,2,128,128]{4,3,2,1,0:T(8,128)} %fusion.2) | copy-start | bytes 6291460
Sparse Core Ops, SparseCore 0:
  8.9 25.2 all-gather.3
  45.9 86.5 all-reduce.4
  135.3 21.5 all-gather.5
  170.7 86.4 all-reduce.6
where the time goes:
time: 267 us
  waiting for transfers between devices  205 us (77%)
  matrix products  21.8 us (8%)
  local copies, waits for them, and re-layouts  21.6 us (8%)
  between operations  13.3 us (5%)
  other arithmetic  4.49 us (2%)
    unnamed x6, waiting for transfers between devices  173 us
    dot_general x6, matrix products, slot_terms(): jnp.einsum('pab,pcudb->cpuad', left_side[:, kslot], selected, precision=H...  21.8 us
    all_gather x1, waiting for transfers between devices, on_device(): gathered = lax.all_gather(density, 'row', axis=0, tiled=True)  20.3 us
    all_gather x1, waiting for transfers between devices, on_device(): square_gathered = lax.all_gather(square, 'row', axis=0, tiled=True)  12 us
    gather x4, local copies, waits for them, and re-layouts, slot_terms(): selected = jnp.take(flat_panel, flat_index[..., kslot], axis=0)  11.8 us
  transfers between devices with their start and end apart: 4, of which 4 were waited for; matrix products, arithmetic and copies ran while one was open for 6% of the time, Pallas kernels for 0%

commit v1 on v0

--- a/solution.py
+++ b/solution.py
@@ -1,6 +1,11 @@
+import functools
+import heapq
+
 import jax
 import jax.numpy as jnp
 from jax import lax
+from jax.experimental import pallas as pl
+from jax.experimental.pallas import tpu as pltpu
 from jax.sharding import PartitionSpec as P
 
 HIGHEST = lax.Precision.HIGHEST
@@ -63,9 +68,247 @@
     return purified.reshape(row_count, 1, slot_count, tile_size, tile_size)
 
 
+SIDE = 4
+PAIRS = tuple((i, j) for i in range(SIDE) for j in range(i, SIDE))
+PARENTS = (
+    (0, 0, 1, 2, 0, 4, 5, 6), (0, 1, 1, 2, 0, 1, 5, 3), (4, 0, 2, 7, 4, 4, 2, 6),
+    (4, 2, 3, 3, 4, 4, 7, 3), (1, 1, 1, 2, 5, 1, 5, 6), (1, 2, 2, 2, 0, 5, 2, 3),
+    (1, 5, 3, 3, 0, 5, 2, 3), (4, 2, 6, 7, 5, 6, 6, 6), (4, 5, 3, 7, 5, 6, 6, 7),
+    (1, 5, 6, 7, 5, 6, 7, 7),
+)
+MESH = pl.DeviceIdType.MESH
+NT = (((1,), (1,)), ((), ()))
+
+
+def orientation(pair, chip):
+    while PARENTS[pair][chip] != chip:
+        chip = PARENTS[pair][chip]
+    i, j = PAIRS[pair]
+    return (i, j) if (i // 2) * SIDE + j == chip else (j, i)
+
+
+def make_plan():
+    heap, free, count = [], {}, 0
+    plan = {(r, c): [] for r in range(SIDE) for c in range(SIDE)}
+
+    def children(pair, chip):
+        return [k for k in range(8) if k != chip and PARENTS[pair][k] == chip]
+
+    def below(pair, chip):
+        return 1 + max([below(pair, k) for k in children(pair, chip)], default=0)
+
+    for pair in range(len(PAIRS)):
+        for chip in range(8):
+            if PARENTS[pair][chip] == chip:
+                i, j = orientation(pair, chip)
+                for row in range(SIDE):
+                    heap.append((0.0, row, -below(pair, chip), count, pair, (i, j), None))
+                    count += 1
+    heapq.heapify(heap)
+    while heap:
+        now, row, _, _, pair, dev, source = heapq.heappop(heap)
+        chip = (dev[0] // 2) * SIDE + dev[1]
+        i, j = orientation(pair, chip)
+        targets = []
+        if source is None or dev[0] % 2 == i % 2:
+            for k in sorted(children(pair, chip), key=lambda k: -below(pair, k)):
+                targets.append((((k // SIDE) * 2 + i % 2, k % SIDE), (chip, k), 1.35))
+            targets.append(((dev[0] ^ 1, dev[1]), dev, 0.3))
+        plan[dev].append((i * SIDE + j, row, source, tuple(t[0] for t in targets)))
+        for target, link, cost in targets:
+            done = max(now, free.get(link, 0.0)) + cost
+            free[link] = done
+            heapq.heappush(heap, (done + 1.0, row, 0, count, pair, target, dev))
+            count += 1
+    return plan
+
+
+def split(value):
+    high = value.astype(jnp.bfloat16)
+    return high, (value - high.astype(jnp.float32)).astype(jnp.bfloat16)
+
+
+def purify_kernel(plan, targets, lookup, mine, out, held, high, low, s32, s_high, s_low, send_sem, recv_sem, own_sem):
+    r, c = lax.axis_index("row"), lax.axis_index("col")
+    chip = (r // 2) * SIDE + c
+    zero = high.shape[0] - 1
+    s_zero = s_high.shape[0] - 1
+
+    def greet(row, col):
+        pl.semaphore_signal(barrier, inc=1, device_id={"row": row, "col": col}, device_id_type=MESH)
+
+    barrier = pltpu.get_barrier_semaphore()
+    greet(r + 1 - 2 * (r % 2), c)
+    greet((r + 2) % SIDE, c)
+
+    @pl.when(c > 0)
+    def _():
+        greet(r, c - 1)
+
+    @pl.when(c < SIDE - 1)
+    def _():
+        greet(r, c + 1)
+
+    edges = (c == 0).astype(jnp.int32) + (c == SIDE - 1).astype(jnp.int32)
+    pl.semaphore_wait(barrier, 4 - edges)
+
+    def remote(slot, row, source, target, number):
+        src = mine if source is None else held.at[slot]
+        return pltpu.make_async_remote_copy(
+            src_ref=src.at[row],
+            dst_ref=held.at[slot, row],
+            send_sem=send_sem.at[number],
+            recv_sem=recv_sem.at[slot, row],
+            device_id={"row": target[0], "col": target[1]},
+            device_id_type=MESH,
+        )
+
+    def on_each_device(action):
+        for dev, steps in plan.items():
+            @pl.when((r == dev[0]) & (c == dev[1]))
+            def _():
+                number = 0
+                for slot, row, source, to in steps:
+                    if action == "run" and source is not None:
+                        remote(slot, row, source, source, 0).wait_recv()
+                    for target in to:
+                        copy = remote(slot, row, source, target, number)
+                        number += 1
+                        if action == "run":
+                            copy.start()
+                        else:
+                            copy.wait_send()
+
+    own = pltpu.make_async_copy(mine, held.at[r * SIDE + c], own_sem)
+    own.start()
+    high[zero] = jnp.zeros_like(high[zero])
+    low[zero] = jnp.zeros_like(low[zero])
+    s_high[s_zero] = jnp.zeros_like(high[zero])
+    s_low[s_zero] = jnp.zeros_like(high[zero])
+    on_each_device("run")
+    own.wait()
+
+    for pair, (i, j) in enumerate(PAIRS):
+        turned = 0
+        for k in range(8):
+            if orientation(pair, k) != (i, j):
+                turned = turned + (chip == k).astype(jnp.int32)
+        first = i + turned * (j - i)
+        second = j - turned * (j - i)
+
+        @pl.loop(0, SIDE)
+        def _(row):
+            for v in range(2):
+                tile = held[first * SIDE + second, row, v]
+                at = ((first * SIDE + row) * SIDE + second) * 2 + v
+                high[at], low[at] = split(tile)
+
+        if i != j:
+            @pl.loop(0, SIDE)
+            def _(row):
+                p = second * SIDE + row
+                for v in range(2):
+                    at = (p * SIDE + first) * 2 + v
+                    source = lookup[targets[at] * 17 + p]
+                    high[at] = high[source].T
+                    low[at] = low[source].T
+
+    def product(x_high, x_low, w_high, w_low):
+        dot = functools.partial(lax.dot_general, dimension_numbers=NT, preferred_element_type=jnp.float32)
+        return dot(x_high, w_high) + dot(x_low, w_high) + dot(x_high, w_low)
+
+    def wide(ref, at):
+        return jnp.concatenate([ref[at], ref[at + 1]], axis=1)
+
+    def gathered(ref, index):
+        return jnp.concatenate(
+            [jnp.concatenate([ref[a] for a in row], axis=1) for row in index], axis=0
+        )
+
+    def rhs_index(p, group, k):
+        tile = (p * SIDE + group) * 2
+        ends = [targets[(p * SIDE + k) * 2 + v] for v in range(2)]
+        return [[lookup[targets[tile + u] * 17 + e] for e in ends] for u in range(2)]
+
+    @pl.loop(0, 8 * SIDE)
+    def _(step):
+        line, group = step // SIDE, step % SIDE
+        second = line // SIDE
+        p = (r + second * (c - r)) * SIDE + line % SIDE
+        total = jnp.zeros((128, 256), jnp.float32)
+        for k in range(SIDE):
+            index = rhs_index(p, group, k)
+            x = (p * SIDE + k) * 2
+            total += product(wide(high, x), wide(low, x), gathered(high, index), gathered(low, index))
+        for u in range(2):
+            at = step * 2 + u
+            tile = total[:, u * 128:(u + 1) * 128]
+            s32[at] = tile
+            s_high[at], s_low[at] = split(tile)
+
+    @pl.loop(0, SIDE)
+    def _(line):
+        p = r * SIDE + line
+        total = jnp.zeros((128, 256), jnp.float32)
+        for k in range(SIDE):
+            index = rhs_index(p, c, k)
+            x = (line * SIDE + k) * 2
+            total += product(wide(s_high, x), wide(s_low, x), gathered(high, index), gathered(low, index))
+            index = [[jnp.where(a == zero, s_zero, jnp.clip(a - c * 32 + 32, 0, s_zero)) for a in row] for row in index]
+            x = (p * SIDE + k) * 2
+            total += product(wide(high, x), wide(low, x), gathered(s_high, index), gathered(s_low, index))
+        for u in range(2):
+            out[line, 0, u] = 3.0 * s32[(line * SIDE + c) * 2 + u] - total[:, u * 128:(u + 1) * 128]
+
+    on_each_device("drain")
+
+
+def on_small_grid(density, slot_cols, block_at):
+    nblocks = slot_cols.shape[0]
+    tiles = nblocks * SIDE * 2
+    order = jnp.arange(nblocks, dtype=jnp.int32)
+    flat = slot_cols.reshape(nblocks, SIDE * 2)
+    targets = jnp.min(jnp.where(flat[..., None] == block_at, order, nblocks), axis=-1)
+    numbers = jnp.arange(tiles, dtype=jnp.int32).reshape(nblocks, SIDE * 2)
+    same = flat[:, None, :] == block_at[None, :, None]
+    lookup = jnp.min(jnp.where(same, numbers[:, None, :], tiles), axis=-1)
+    lookup = jnp.pad(lookup, ((0, 1), (0, 1)), constant_values=tiles)
+    tile_shape = (128, 128)
+    return pl.pallas_call(
+        functools.partial(purify_kernel, make_plan()),
+        out_shape=jax.ShapeDtypeStruct(density.shape, jnp.float32),
+        in_specs=[
+            pl.BlockSpec(memory_space=pltpu.SMEM),
+            pl.BlockSpec(memory_space=pltpu.SMEM),
+            pl.BlockSpec(memory_space=pltpu.VMEM),
+        ],
+        out_specs=pl.BlockSpec(memory_space=pltpu.VMEM),
+        scratch_shapes=[
+            pltpu.VMEM((16, SIDE, 2) + tile_shape, jnp.float32),
+            pltpu.VMEM((tiles + 1,) + tile_shape, jnp.bfloat16),
+            pltpu.VMEM((tiles + 1,) + tile_shape, jnp.bfloat16),
+            pltpu.VMEM((64,) + tile_shape, jnp.float32),
+            pltpu.VMEM((65,) + tile_shape, jnp.bfloat16),
+            pltpu.VMEM((65,) + tile_shape, jnp.bfloat16),
+            pltpu.SemaphoreType.DMA((64,)),
+            pltpu.SemaphoreType.DMA((16, SIDE)),
+            pltpu.SemaphoreType.DMA,
+        ],
+        compiler_params=pltpu.CompilerParams(
+            collective_id=0, has_side_effects=True, vmem_limit_bytes=48 * 2**20
+        ),
+        cost_estimate=pl.CostEstimate(flops=7 * 10**9, bytes_accessed=2**20, transcendentals=0),
+    )(targets.reshape(-1), lookup.reshape(-1), density.reshape(SIDE, 2, *tile_shape)).reshape(density.shape)
+
+
 def solution(mesh):
     in_specs = (P(("grp", "row"), "col", None, None, None), P("grp", None, None), P("grp"))
     out_specs = P(("grp", "row"), "col", None, None, None)
+    small = mesh.shape["row"] == SIDE and mesh.shape["col"] == SIDE
     return jax.shard_map(
-        on_device, mesh=mesh, in_specs=in_specs, out_specs=out_specs, check_vma=False
+        on_small_grid if small else on_device,
+        mesh=mesh,
+        in_specs=in_specs,
+        out_specs=out_specs,
+        check_vma=False,
     )

time: 267 us -> 67.6 us (0.25)
  waiting for transfers between devices: 205 us -> 0 us
  Pallas kernels: 0 us -> 64.1 us
  matrix products: 21.8 us -> 0 us
  local copies, waits for them, and re-layouts: 21.6 us -> 2.78 us
  between operations: 13.3 us -> 0.05 us
  other arithmetic: 4.49 us -> 0.53 us
    unnamed x6 -> x0, waiting for transfers between devices: 173 us -> none
    pallas_call x0 -> x1, Pallas kernels: none -> 64.1 us  [on_small_grid(): pl.pallas_call(functools.partial(purify_kernel, make_plan()), out_shape=j...]
    all_gather x2 -> x0, waiting for transfers between devices: 32.3 us -> none  [the longest x1 20.3 us: on_device(): gathered = lax.all_gather(density, 'row', axis=0, tiled=True)]
    dot_general x6 -> x0, matrix products: 21.8 us -> none  [slot_terms(): jnp.einsum('pab,pcudb->cpuad', left_side[:, kslot], selected, precision=H...]
    gather x6 -> x0, local copies, waits for them, and re-layouts: 12.5 us -> none  [the longest x4 11.8 us: slot_terms(): selected = jnp.take(flat_panel, flat_index[..., kslot], axis=0)]
  transfers between devices with their start and end apart: 4 -> 0, of which waited for: 4 -> 0; matrix products, arithmetic and copies ran while one was open for 6% -> 0% of each run, Pallas kernels for 0% -> 0%
where the time goes in v1:
time: 67.6 us; the launch traced here: 67.4 us
  Pallas kernels  64.1 us (95%)
  local copies, waits for them, and re-layouts  2.78 us (4%)
    pallas_call x1, Pallas kernels, on_small_grid(): pl.pallas_call(functools.partial(purify_kernel, make_plan()), out_shape=j...  64.1 us
    unnamed x5, local copies, waits for them, and re-layouts  1.84 us

profile of v1, /device:TPU:0, one launch (start us, length us, event | category | flops | bytes accessed | tf_op | source)
XLA Modules:
  0.0 67.4 jit_solution(10416873489685792914)
XLA Ops:
  0.0 0.0 copy-start.1
  0.0 0.8 %copy.8 = s32[16,8]{1,0:T(8,128)S(1)} copy(s32[16,8]{0,1:T(8,128)} %bitcast.3) | data formatting | bytes 1024 | tf_op jit(solution)/shard_map/eq | solution.py:271
  0.8 0.0 copy-done.1
  0.8 0.4 select_reduce_fusion.1
  1.2 0.1 reshape.26.targets
  1.3 0.1 select_reduce_fusion
  1.4 0.1 reshape.27.lookup
  1.5 0.0 copy-start
  1.5 1.0 %copy-done = f32[4,1,2,128,128]{4,3,2,1,0:T(8,128)S(1)} copy-done((f32[4,1,2,128,128]{4,3,2,1,0:T(8,128)S(1)}, f32[4,1,2,128,128]{4,3,2,1,0:T(8,128)}, u32[]{:S(2)}) %copy-start) | copy-done | bytes 524312
  2.6 64.1 %shard_map.37 = f32[4,1,2,128,128]{4,3,2,1,0:T(8,128)S(1)} custom-call(s32[128]{0:T(128)S(1)} %reshape.26.targets, s32[289]{0:T(512)S(1)} %reshape.27.lookup, f32[4,2,128,128]{3,2,1,0:T(8,128)S(1)} %bitcast.2), custom_call_target="tpu_custom_call" | custom-call | flops 7000000000 | bytes 1048576 | tf_op jit(solution)/shard_map/pallas_call | solution.py:277
  66.6 0.8 %copy.11 = f32[4,1,2,128,128]{4,3,2,1,0:T(8,128)} copy(f32[4,1,2,128,128]{4,3,2,1,0:T(8,128)S(1)} %shard_map.37) | data formatting | bytes 1048576
  (2 shorter events, 0.0 us)
Async XLA Ops:
  0.0 0.8 %copy-start.1 = (s32[16]{0:T(128)S(1)}, s32[16]{0:T(128)}, u32[]{:S(2)}) copy-start(s32[16]{0:T(128)} %param.5) | copy-start | bytes 196
  1.5 1.0 %copy-start = (f32[4,1,2,128,128]{4,3,2,1,0:T(8,128)S(1)}, f32[4,1,2,128,128]{4,3,2,1,0:T(8,128)}, u32[]{:S(2)}) copy-start(f32[4,1,2,128,128]{4,3,2,1,0:T(8,128)} %param.3) | copy-start | bytes 1572868
